TPU v7x, 32 devices: a whole 2x2x4 slice. The times are simulated.
32 devices in a mesh: grp: 2 (over x), img: 16 (over z, y, core).
Axes of the slice: x: 2, y: 2, z: 4, core: 2. Of those that a mesh axis runs over, the one named last changes fastest.
Arguments:
- particles: bfloat16 [64, 256, 512], P(('grp', 'img')), parts along dimension 0, may hold values from -6 to 6
- whitening: float32 [256], replicated, may hold values from 0.5 to 2
- ctf: float32 [16, 256], P('grp'), parts along dimension 0, may hold values from -1 to 1
- group_id: int32 [64], P(('grp', 'img')), parts along dimension 0, may hold values from 0 to 7
- noise_var: float32 [16], P('grp'), parts along dimension 0, may hold values from 0.1 to 1
- bessel: bfloat16 [128, 64, 256], replicated, may hold values from -0.375 to 0.375
Outputs:
- cleaned: bfloat16 [64, 256, 512], P(('grp', 'img')), parts along dimension 0
There are 2 independent parts, one for each index of `grp`. A program takes and returns all parts, laid end to end along the dimension named above; an argument that names none is the same for every part. Nothing has to cross between parts.
All inputs are finite; a program needn't handle non-finite values.
Results may differ from a plain program's by a relative error of at most 0.0087.
Values may be sent and summed in bfloat16 or wider, within the bound.
A program may use at most 64 MiB of HBM per device.

v0:
```python
import math

import jax
import jax.numpy as jnp
from jax import lax
from jax.sharding import PartitionSpec as P

prior_weight = 8.0


def angle_table(angles, freqs):
    theta = jnp.arange(angles, dtype=jnp.int32)
    order = jnp.arange(freqs, dtype=jnp.int32)
    phase = 2.0 * math.pi / angles * (theta[:, None] * order[None, :] % angles).astype(jnp.float32)
    scale = 1.0 / math.sqrt(angles)
    return jnp.stack([jnp.cos(phase) * scale, -jnp.sin(phase) * scale], axis=1).astype(jnp.bfloat16)


def filter_block(block, labels, counts, noise_var):
    radial = block.shape[-1]
    groups = labels.shape[1]
    rows = block.reshape(-1, radial)
    spread = (rows[:, None, :] * labels[:, :, None]).reshape(rows.shape[0], groups * radial)
    gram = lax.dot_general(
        spread, rows, (((0,), (0,)), ((), ())), preferred_element_type=jnp.float32
    )
    gram = gram.reshape(groups, radial, radial)
    pooled = jnp.sum(gram, axis=0) / (rows.shape[0] // 2)
    cov = (gram + prior_weight * pooled[None]) / (counts + prior_weight)[:, None, None]
    eye = jnp.eye(radial, dtype=jnp.float32)
    system = cov + noise_var[:, None, None] * eye[None]
    factor = jnp.linalg.cholesky(system)
    lower_inv = lax.linalg.triangular_solve(
        factor, jnp.broadcast_to(eye, system.shape), left_side=True, lower=True
    )
    inverse = jnp.einsum("gsq,gst->gqt", lower_inv, lower_inv, precision=lax.Precision.HIGHEST)
    wiener = (eye[None] - noise_var[:, None, None] * inverse).astype(jnp.bfloat16)
    weights = wiener.transpose(2, 0, 1).reshape(radial, groups * radial)
    mixed = jnp.dot(rows, weights, preferred_element_type=jnp.float32).reshape(
        rows.shape[0], groups, radial
    )
    applied = jnp.sum(mixed * labels.astype(jnp.float32)[:, :, None], axis=1).astype(jnp.bfloat16)
    return applied.reshape(block.shape)


def body(particles, whitening, ctf, group_id, noise_var, bessel):
    img_count, radii, angles = particles.shape
    freqs = bessel.shape[0]
    groups = ctf.shape[0]
    shards = lax.axis_size("img")
    per_shard = freqs // shards
    group_range = jnp.arange(groups, dtype=jnp.int32)
    onehot_local = (group_id[:, None] == group_range[None, :]).astype(jnp.float32)
    weight_rows = jnp.dot(onehot_local, ctf, precision=lax.Precision.HIGHEST) * whitening[None, :]
    filtered = (particles.astype(jnp.float32) * weight_rows[:, :, None]).astype(jnp.bfloat16)
    table = angle_table(angles, freqs)
    spectrum = jnp.dot(
        filtered.reshape(img_count * radii, angles),
        table.reshape(angles, 2 * freqs),
        preferred_element_type=jnp.float32,
    )
    spectrum = spectrum.astype(jnp.bfloat16).reshape(img_count, radii, 2, freqs)
    all_ids = lax.all_gather(group_id, "img", axis=0, tiled=True)
    onehot_all = (all_ids[:, None] == group_range[None, :]).astype(jnp.float32)
    counts = jnp.sum(onehot_all, axis=0)
    labels = jnp.repeat(onehot_all, 2, axis=0).astype(jnp.bfloat16)
    first = lax.axis_index("img") * per_shard
    own_tables = lax.dynamic_slice_in_dim(bessel, first, per_shard, 0)
    payload = spectrum.transpose(3, 0, 2, 1)
    arrived = lax.all_to_all(payload, "img", split_axis=0, concat_axis=1, tiled=True)
    coef = jnp.einsum(
        "kipr,kqr->kipq", arrived, own_tables, preferred_element_type=jnp.float32
    ).astype(jnp.bfloat16)
    denoised = jax.vmap(lambda block: filter_block(block, labels, counts, noise_var))(coef)
    outgoing = jnp.einsum(
        "kipq,kqr->kipr", denoised, own_tables, preferred_element_type=jnp.float32
    ).astype(jnp.bfloat16)
    returned = lax.all_to_all(outgoing, "img", split_axis=1, concat_axis=0, tiled=True)
    back = returned.transpose(1, 3, 2, 0)
    cleaned = jnp.dot(
        back.reshape(img_count * radii, 2 * freqs),
        table.reshape(angles, 2 * freqs).T,
        preferred_element_type=jnp.float32,
    )
    return cleaned.astype(jnp.bfloat16).reshape(img_count, radii, angles)


def solution(mesh):
    in_specs = (
        P(("grp", "img"), None, None),
        P(),
        P("grp", None),
        P(("grp", "img")),
        P("grp"),
        P(),
    )
    out_specs = P(("grp", "img"), None, None)
    return jax.shard_map(body, mesh=mesh, in_specs=in_specs, out_specs=out_specs, check_vma=False)
```

profile of v0, /device:TPU:0, one launch (start us, length us, event | category | flops | bytes accessed | tf_op | source)
XLA Modules:
  0.0 759.7 jit_solution(12604015200932532926)
XLA Ops:
  0.0 1.1 multiply_convert_fusion.1
  1.4 1.0 convolution_multiply_fusion
  2.3 1.2 multiply_convert_fusion
  4.0 1.0 copy.102
  5.0 7.4 all-to-all-start
  12.4 0.6 dynamic-slice
  13.9 12.4 %all-reduce = s32[32]{0:T(128)S(1)} all-reduce(s32[32]{0:T(128)S(1)} %dynamic-update-slice.3), channel_id=1, replica_groups=mesh['grp'=2,'img'=16] {'img'}, use_global_device_ids=true, to_apply=%add | all-reduce | flops 32 | bytes 256
  26.5 0.6 iota_compare_fusion
  27.1 0.6 fusion.23
  29.8 1.2 convolution_convert_fusion.3
  31.3 0.6 mul.170
  32.7 0.6 reduce_sum.27
  33.4 1.8 fusion.5
  35.2 2.9 copy.110
  38.1 3.6 fusion.3
  41.7 375.7 %custom-call.7 = f32[8,8,64,64]{3,2,1,0:T(8,128)S(1)} custom-call(f32[8,8,64,64]{3,2,1,0:T(8,128)} %fusion.3), custom_call_target="Cholesky" | custom-call | tf_op jit(solution)/shard_map/vmap(jit(cholesky))/cholesky | solution.py:32
  418.0 1.7 select_bitcast_fusion
  419.7 315.4 %custom-call.8 = f32[8,8,1,64,64]{3,4,2,1,0:T(8,128)S(1)} custom-call(f32[8,8,1,64,64]{4,3,2,1,0:T(8,128)} %select_bitcast_fusion), custom_call_target="InvertDiagBlocksLowerTriangular" | custom-call | tf_op jit(solution)/shard_map/vmap()/triangular_solve | solution.py:33
  735.1 3.5 fusion.1
  738.6 3.6 fusion
  743.5 0.7 multiply_reduce_fusion
  744.2 1.2 convolution_convert_fusion.1
  745.7 12.6 %all_to_all.36 = bf16[8,32,2,256]{3,2,0,1:T(2,128)(2,1)S(1)} all-to-all(bf16[8,32,2,256]{3,2,0,1:T(2,128)(2,1)S(1)} %copy.117), channel_id=1, replica_groups=mesh['grp'=2,'img'=16] {'img'}, dimensions={1} | all-to-all | bytes 524288 | tf_op jit(solution)/shard_map/all_to_all | solution.py:78
  758.6 1.1 convolution_convert_fusion
  (61 shorter events, 6.4 us)
Async XLA Ops:
  0.0 1.3 copy-start
  1.2 11.2 %copy-start.12 = (u32[32]{0:T(128)S(1)}, u32[32]{0:T(128)}, u32[]{:S(2)}) copy-start(u32[32]{0:T(128)} %constant.86) | copy-start | bytes 388
  1.2 12.5 %copy-start.11 = (s32[2]{0:T(128)S(1)}, s32[2]{0:T(128)}, u32[]{:S(2)}) copy-start(s32[2]{0:T(128)} %param.9) | copy-start | bytes 28
  1.3 27.3 %copy-start.1 = (bf16[512,2,128]{0,2,1:T(8,128)(2,1)}, bf16[512,2,128]{0,2,1:T(8,128)(2,1)S(1)}, u32[]{:S(2)}) copy-start(bf16[512,2,128]{0,2,1:T(8,128)(2,1)S(1)} %copy.101) | copy-start | bytes 786436
  2.3 27.0 %copy-start.9 = (f32[8]{0:T(128)S(1)}, f32[8]{0:T(128)}, u32[]{:S(2)}) copy-start(f32[8]{0:T(128)} %param.10) | copy-start | bytes 100
  5.0 24.4 %all-to-all-start = ((bf16[128,2,2,256]{3,2,1,0:T(2,128)(2,1)}), bf16[128,2,2,256]{3,2,1,0:T(2,128)(2,1)S(1)}, u32[]{:S(2)}, u32[]{:S(2)}) async-start(bf16[128,2,2,256]{3,2,1,0:T(2,128)(2,1)} %bitcast.2), calls=%async_computation | async-start | bytes 524288 | tf_op jit(solution)/shard_map/all_to_all | solution.py:70
  26.5 3.0 copy-start.3
  32.7 0.7 copy-start.8
  38.1 379.3 %copy-start.7 = (pred[64,64]{1,0:T(8,128)(4,1)S(1)}, pred[64,64]{1,0:T(8,128)(4,1)}, u32[]{:S(2)}) copy-start(pred[64,64]{1,0:T(8,128)(4,1)} %iota_compare_fusion) | copy-start | bytes 12292
  418.0 317.1 %copy-start.4 = (f32[64,64]{1,0:T(8,128)S(1)}, f32[64,64]{1,0:T(8,128)}, u32[]{:S(2)}) copy-start(f32[64,64]{1,0:T(8,128)} %copy-done.3) | copy-start | bytes 49156
  735.1 3.5 copy-start.5
  735.1 3.5 copy-start.10
  742.7 0.8 copy-start.6
  744.2 14.4 %copy-start.2 = (bf16[512,2,128]{0,2,1:T(8,128)(2,1)S(1)}, bf16[512,2,128]{0,2,1:T(8,128)(2,1)}, u32[]{:S(2)}) copy-start(bf16[512,2,128]{0,2,1:T(8,128)(2,1)} %copy-done.1) | copy-start | bytes 786436
where the time goes:
time: 760 us
  other arithmetic  705 us (93%)
  blocking collectives  25 us (3%)
  matrix products  12.7 us (2%)
  local copies, waits for them, and re-layouts  8.32 us (1%)
    another operation x3, other arithmetic, filter_block(): factor = jnp.linalg.cholesky(system)  376 us
    another operation x3, other arithmetic, filter_block(): lax.linalg.triangular_solve(factor, jnp.broadcast_to(eye, system.shape),...  317 us
  transfers between devices with their start and end apart: 1, of which 0 were waited for; matrix products, arithmetic and copies ran while one was open for 1% of the time, Pallas kernels for 0%

commit v1 on v0

v1 whole, which is shorter than its diff:
```python
import functools
import math

import jax
import jax.numpy as jnp
from jax import lax
from jax.experimental import pallas as pl
from jax.experimental.pallas import tpu as pltpu
from jax.sharding import PartitionSpec as P

prior_weight = 8.0
SLOTS = 64
LANES = 2 * SLOTS
TILE = 8


def angle_table(angles, freqs):
    theta = jnp.arange(angles, dtype=jnp.int32)
    order = jnp.arange(freqs, dtype=jnp.int32)
    phase = 2.0 * math.pi / angles * (theta[:, None] * order[None, :] % angles).astype(jnp.float32)
    scale = 1.0 / math.sqrt(angles)
    return jnp.stack([jnp.cos(phase) * scale, -jnp.sin(phase) * scale], axis=1).astype(jnp.bfloat16)


def nt_dot(a, b):
    return lax.dot_general(a, b, (((1,), (1,)), ((), ())), preferred_element_type=jnp.float32)


def swap_halves(x):
    return pltpu.roll(x, SLOTS, x.ndim - 1)


def sweep_all(a_ref, c_ref, v_ref, q):
    hq = q // 2
    half = lax.broadcasted_iota(jnp.int32, (TILE, LANES), 1) // SLOTS
    half_w = lax.broadcasted_iota(jnp.int32, (hq, LANES), 1) // SLOTS
    sub_w = lax.broadcasted_iota(jnp.int32, (hq, LANES), 0)
    for kb in range(q // TILE):
        h, base = divmod(kb * TILE, hq)
        in_half = half == h
        rows = [a_ref[kb * TILE + t] for t in range(TILE)]
        for t in range(TILE):
            row = rows[t]
            turned = swap_halves(row)
            c_ref[t, 0:hq] = jnp.where(half_w == 0, row, turned)
            c_ref[t, hq:q] = jnp.where(half_w == 1, row, turned)
            own = jnp.where(in_half, row[base:base + TILE], turned[base:base + TILE])
            inv = 1.0 / own[t:t + 1]
            here = (half_w == h) & (sub_w == base + t)
            scaled = jnp.where(here, -inv, row * inv)
            later = (half_w == h) & (sub_w > base + t) & (sub_w < base + TILE)
            v_ref[t] = jnp.where(later, 0.0, scaled)
            for u in range(TILE):
                if u != t:
                    rows[u] = jnp.where(here, 0.0, rows[u]) - own[u:u + 1] * scaled
            rows[t] = scaled
        vs = [v_ref[t] for t in range(TILE)]
        keep = ~((half_w == h) & (sub_w >= base) & (sub_w < base + TILE))

        def update(i, carry):
            acc = jnp.where(keep, a_ref[i], 0.0)
            for t in range(TILE):
                acc = acc - c_ref[t, pl.ds(i, 1), :] * vs[t]
            a_ref[i] = acc
            return carry

        lax.fori_loop(0, q, update, 0, unroll=4)
        for t in range(TILE):
            a_ref[kb * TILE + t] = rows[t]


def filter_kernel(groups, imgs, coef_ref, bid_ref, kid_ref, noise_ref, out_ref, cf_ref, a_ref, c_ref, v_ref, d_ref):
    q, width = coef_ref.shape
    hq = q // 2
    slot = lax.broadcasted_iota(jnp.int32, (LANES, width), 0)
    member = (slot % SLOTS == bid_ref[...]).astype(jnp.float32)
    same = (slot % SLOTS // groups == kid_ref[...]).astype(jnp.float32)
    low = slot < SLOTS
    weights = member + same * (prior_weight / imgs)
    w_lo = jnp.where(low, weights, 0.0).astype(jnp.bfloat16)
    w_hi = jnp.where(low, 0.0, weights).astype(jnp.bfloat16)
    counts = nt_dot(jnp.full((TILE, width), 0.5, jnp.bfloat16), member.astype(jnp.bfloat16))[0:1]
    scale = 1.0 / (counts + prior_weight)
    noise = noise_ref[...]
    cf_ref[...] = coef_ref[...].astype(jnp.float32)
    jj = lax.broadcasted_iota(jnp.int32, (hq, LANES), 0)
    col = jj + hq * (lax.broadcasted_iota(jnp.int32, (hq, LANES), 1) // SLOTS)

    def gram(blk, carry):
        start = pl.multiple_of(blk * TILE, TILE)
        mine = cf_ref[pl.ds(start, TILE), :]
        total = None
        for part, w in ((0, w_lo), (1, w_hi)):
            other = cf_ref[part * hq:(part + 1) * hq, :]
            prod = (mine[:, None, :] * other[None, :, :]).reshape(TILE * hq, width)
            top = prod.astype(jnp.bfloat16)
            rest = (prod - top.astype(jnp.float32)).astype(jnp.bfloat16)
            s = nt_dot(top, w) + nt_dot(rest, w)
            total = s if total is None else total + s
        total = total.reshape(TILE, hq, LANES) * scale[None]
        for t in range(TILE):
            a_ref[start + t] = total[t] + jnp.where(col == start + t, noise, 0.0)
        return carry

    lax.fori_loop(0, q // TILE, gram, 0)
    sweep_all(a_ref, c_ref, v_ref, q)
    e_lo = jnp.where(low, member, 0.0).astype(jnp.bfloat16)
    e_hi = jnp.where(low, 0.0, member).astype(jnp.bfloat16)

    def apply(blk, carry):
        start = pl.multiple_of(blk * TILE, TILE)
        wien = []
        for t in range(TILE):
            wien.append(noise * a_ref[start + t] + jnp.where(col == start + t, 1.0, 0.0))
        wien = jnp.concatenate(wien, axis=0).astype(jnp.bfloat16)
        spread_lo = jnp.dot(wien, e_lo, preferred_element_type=jnp.float32).reshape(TILE, hq, width)
        spread_hi = jnp.dot(wien, e_hi, preferred_element_type=jnp.float32).reshape(TILE, hq, width)
        prod = spread_lo * cf_ref[0:hq, :][None] + spread_hi * cf_ref[hq:q, :][None]
        d_ref[pl.ds(start, TILE), :] = jnp.sum(prod, axis=1)
        return carry

    lax.fori_loop(0, q // TILE, apply, 0)
    out_ref[...] = d_ref[...].astype(jnp.bfloat16)


def wiener_filter(coef, bid, kid, noise, groups, imgs):
    q, width = coef.shape
    hq = q // 2
    return pl.pallas_call(
        functools.partial(filter_kernel, groups, imgs),
        out_shape=jax.ShapeDtypeStruct((q, width), jnp.bfloat16),
        in_specs=[pl.BlockSpec(memory_space=pltpu.VMEM)] * 4,
        out_specs=pl.BlockSpec(memory_space=pltpu.VMEM),
        scratch_shapes=[
            pltpu.VMEM((q, width), jnp.float32),
            pltpu.VMEM((q, hq, LANES), jnp.float32),
            pltpu.VMEM((TILE, q, LANES), jnp.float32),
            pltpu.VMEM((TILE, hq, LANES), jnp.float32),
            pltpu.VMEM((q, width), jnp.float32),
        ],
        compiler_params=pltpu.CompilerParams(vmem_limit_bytes=32 * 1024 * 1024),
        name="wiener_filter",
    )(coef, bid, kid, noise)


def body(particles, whitening, ctf, group_id, noise_var, bessel):
    img_count, radii, angles = particles.shape
    freqs, radial = bessel.shape[:2]
    groups = ctf.shape[0]
    shards = lax.axis_size("img")
    per_shard = freqs // shards
    imgs = shards * img_count
    group_range = jnp.arange(groups, dtype=jnp.int32)
    onehot_local = (group_id[:, None] == group_range[None, :]).astype(jnp.float32)
    weight_rows = jnp.dot(onehot_local, ctf, precision=lax.Precision.HIGHEST) * whitening[None, :]
    filtered = (particles.astype(jnp.float32) * weight_rows[:, :, None]).astype(jnp.bfloat16)
    table = angle_table(angles, freqs)
    spectrum = jnp.dot(
        filtered.reshape(img_count * radii, angles),
        table.reshape(angles, 2 * freqs),
        preferred_element_type=jnp.float32,
    )
    spectrum = spectrum.astype(jnp.bfloat16).reshape(img_count, radii, 2, freqs)
    all_ids = lax.all_gather(group_id, "img", axis=0, tiled=True)
    first = lax.axis_index("img") * per_shard
    own_tables = lax.dynamic_slice_in_dim(bessel, first, per_shard, 0)
    payload = spectrum.transpose(3, 0, 2, 1)
    arrived = lax.all_to_all(payload, "img", split_axis=0, concat_axis=1, tiled=True)
    coef = jnp.einsum(
        "kqr,kipr->qkip", own_tables, arrived, preferred_element_type=jnp.float32
    ).astype(jnp.bfloat16)
    kid = jnp.repeat(jnp.arange(per_shard, dtype=jnp.int32), 2 * imgs)[None, :]
    bid = kid * groups + jnp.tile(jnp.repeat(all_ids, 2), per_shard)[None, :]
    noise = jnp.tile(noise_var, LANES // groups)[None, :]
    denoised = wiener_filter(
        coef.reshape(radial, per_shard * 2 * imgs), bid, kid, noise, groups, imgs
    ).reshape(radial, per_shard, imgs, 2)
    outgoing = jnp.einsum(
        "qkip,kqr->kipr", denoised, own_tables, preferred_element_type=jnp.float32
    ).astype(jnp.bfloat16)
    returned = lax.all_to_all(outgoing, "img", split_axis=1, concat_axis=0, tiled=True)
    back = returned.transpose(1, 3, 2, 0)
    cleaned = jnp.dot(
        back.reshape(img_count * radii, 2 * freqs),
        table.reshape(angles, 2 * freqs).T,
        preferred_element_type=jnp.float32,
    )
    return cleaned.astype(jnp.bfloat16).reshape(img_count, radii, angles)


def solution(mesh):
    in_specs = (
        P(("grp", "img"), None, None),
        P(),
        P("grp", None),
        P(("grp", "img")),
        P("grp"),
        P(),
    )
    out_specs = P(("grp", "img"), None, None)
    return jax.shard_map(body, mesh=mesh, in_specs=in_specs, out_specs=out_specs, check_vma=False)
```

time: 760 us -> 61.7 us (0.08)
  other arithmetic: 705 us -> 2.37 us
  Pallas kernels: 0 us -> 17.3 us
  matrix products: 12.7 us -> 4.64 us
    another operation x7 -> x1, other arithmetic: 694 us -> 1.11 us  [the longest x3 376 us: filter_block(): factor = jnp.linalg.cholesky(system)]
    pallas_call x0 -> x1, Pallas kernels: none -> 17.3 us  [wiener_filter(): pl.pallas_call(functools.partial(filter_kernel, groups, imgs), out_shape=...]
  transfers between devices with their start and end apart: 1 -> 1, of which waited for: 0 -> 0; matrix products, arithmetic and copies ran while one was open for 1% -> 2% of each run, Pallas kernels for 0% -> 0%
where the time goes in v1:
time: 61.7 us; the launch traced here: 61.3 us
  blocking collectives  25.1 us (41%)
  Pallas kernels  17.3 us (28%)
  starting transfers between devices  7.39 us (12%)
  matrix products  4.64 us (8%)
  local copies, waits for them, and re-layouts  3.69 us (6%)
  other arithmetic  2.37 us (4%)
  between operations  0.84 us (1%)
    pallas_call x1, Pallas kernels, wiener_filter(): pl.pallas_call(functools.partial(filter_kernel, groups, imgs), out_shape=...  17.3 us
    all_to_all x1, blocking collectives, body(): lax.all_to_all(outgoing, 'img', split_axis=1, concat_axis=0, tiled=True)  12.6 us
    unnamed x1, blocking collectives  12.4 us
    all_to_all x1, starting transfers between devices, body(): lax.all_to_all(payload, 'img', split_axis=0, concat_axis=1, tiled=True)  7.39 us
  transfers between devices with their start and end apart: 1, of which 0 were waited for; matrix products, arithmetic and copies ran while one was open for 2% of the time, Pallas kernels for 0%

profile of v1, /device:TPU:0, one launch (start us, length us, event | category | flops | bytes accessed | tf_op | source)
XLA Modules:
  0.0 61.3 jit_solution(8685397725140202868)
XLA Ops:
  0.0 1.1 %multiply_convert_fusion.1 = (bf16[512,1,128]{2,0,1:T(8,128)(2,1)S(1)}, bf16[512,1,128]{2,0,1:T(8,128)(2,1)S(1)}) fusion(), kind=kLoop, calls=%fused_computation.20 | loop fusion | flops 1245184 | bytes 262144 | tf_op jit(solution)/shard_map/convert.1
  1.2 0.1 copy.49
  1.3 0.9 %convolution_multiply_fusion = f32[2,256]{1,0:T(2,128)S(1)} fusion(f32[8,256]{1,0:T(8,128)S(1)} %copy-done, f32[256]{0:T(256)} %param.7, s32[2]{0:T(128)} %param.9), kind=kOutput, calls=%fused_computation.5 | convolution fusion | flops 49680 | bytes 11272 | tf_op jit(solution)/shard_map/dot_general | solution.py:155
  2.2 1.2 %multiply_convert_fusion = bf16[2,256,512]{2,1,0:T(8,128)(2,1)S(1)} fusion(bf16[2,256,512]{2,1,0:T(8,128)(2,1)} %param.6, f32[2,256]{1,0:T(2,128)S(1)} %convolution_multiply_fusion), kind=kLoop, calls=%fused_computation.6 | loop fusion | flops 786432 | bytes 1050624 | tf_op jit(solution)/shard_map/convert_element_type | solution.py:156
  3.4 0.3 convolution_convert_fusion.2
  3.9 1.0 %copy.50 = bf16[2,256,2,128]{1,2,0,3:T(2,128)(2,1)} copy(bf16[2,256,2,128]{3,2,1,0:T(2,128)(2,1)S(1)} %reshape.137) | data formatting | bytes 524288 | tf_op jit(solution)/shard_map/reshape | solution.py:163
  4.8 7.4 %all-to-all-start = ((bf16[128,2,2,256]{3,2,1,0:T(2,128)(2,1)}), bf16[128,2,2,256]{3,2,1,0:T(2,128)(2,1)S(1)}, u32[]{:S(2)}, u32[]{:S(2)}) async-start(bf16[128,2,2,256]{3,2,1,0:T(2,128)(2,1)} %bitcast.2), calls=%async_computation | async-start | bytes 524288 | tf_op jit(solution)/shard_map/all_to_all | solution.py:168
  12.3 0.6 dynamic-slice
  13.5 0.2 dynamic-update-slice
  13.7 12.4 %all-reduce = s32[32]{0:T(128)S(1)} all-reduce(s32[32]{0:T(128)S(1)} %dynamic-update-slice), channel_id=1, replica_groups=mesh['grp'=2,'img'=16] {'img'}, use_global_device_ids=true, to_apply=%add | all-reduce | flops 32 | bytes 256
  26.2 0.1 tile.6
  26.5 0.1 broadcast_in_dim_tile.7.noise_ref
  26.7 0.3 copy.52
  26.9 0.1 all_to_all.29
  27.1 1.2 %fusion = bf16[64,8,32,2]{0,2,3,1:T(8,128)(2,1)S(1)} fusion(bf16[8,32,2,256]{3,1,2,0:T(8,128)(2,1)S(1)} %all_to_all.29, bf16[128,64,256]{2,1,0:T(8,128)(2,1)} %param.11, s32[]{:T(128)S(6)} %select_n.24), kind=kOutput, calls=%fused_computation.4 | convolution fusion | flops 16809984 | bytes 589828 | tf_op jit(solution)/shard_map/kqr,kipr->qkip/dot_general | solution.py:169
  28.2 0.1 copy.53
  28.4 0.1 copy.54.coef_ref
  28.5 17.3 %wiener_filter.1 = bf16[64,512]{1,0:T(8,128)(2,1)S(1)} custom-call(bf16[64,512]{1,0:T(8,128)(2,1)S(1)} %copy.54.coef_ref, s32[1,512]{1,0:T(1,128)S(1)} %multiply_add_fusion.bid_ref, s32[1,512]{1,0:T(1,128)S(1)} %broadcast_in_dim_reshape.5.kid_ref, f32[1,128]{1,0:T(1,128)S(1)} %broadcast_in_dim_tile.7.noise_ref), custom_call_target="tpu_custom_call" | custom-call | tf_op jit(solution)/shard_map/wiener_filter/pallas_call | solution.py:129
  45.8 0.1 copy.55
  45.9 1.2 %convolution_convert_fusion.1 = bf16[8,32,2,256]{3,1,2,0:T(8,128)(2,1)S(1)} fusion(bf16[128,64,256]{2,1,0:T(8,128)(2,1)} %param.11, s32[]{:T(128)S(6)} %select_n.24, bf16[64,8,32,2]{0,3,2,1:T(2,128)(2,1)S(1)} %bitcast.49), kind=kOutput, calls=%fused_computation.1 | convolution fusion | flops 16908288 | bytes 589828 | tf_op jit(solution)/shard_map/qkip,kqr->kipr/dot_general | solution.py:178
  47.1 0.3 copy.57
  47.4 12.6 %all_to_all.36 = bf16[8,32,2,256]{3,2,0,1:T(2,128)(2,1)S(1)} all-to-all(bf16[8,32,2,256]{3,2,0,1:T(2,128)(2,1)S(1)} %copy.57), channel_id=1, replica_groups=mesh['grp'=2,'img'=16] {'img'}, dimensions={1} | all-to-all | bytes 524288 | tf_op jit(solution)/shard_map/all_to_all | solution.py:181
  60.1 0.2 copy.60
  60.2 1.1 %convolution_convert_fusion = bf16[512,512]{1,0:T(8,128)(2,1)} fusion(bf16[512,256]{0,1:T(8,128)(2,1)S(1)} %bitcast.42, bf16[64,8,2,128]{3,2,1,0:T(2,128)(2,1)S(1)} %bitcast.47), kind=kOutput, calls=%fused_computation | convolution fusion | flops 134479872 | bytes 1048576 | tf_op jit(solution)/shard_map/dot_general | solution.py:183
  (22 shorter events, 0.4 us)
Async XLA Ops:
  0.0 1.3 %copy-start = (f32[8,256]{1,0:T(8,128)S(1)}, f32[8,256]{1,0:T(8,128)}, u32[]{:S(2)}) copy-start(f32[8,256]{1,0:T(8,128)} %param.8) | copy-start | bytes 24580
  0.0 12.2 %copy-start.3 = (u32[32]{0:T(128)S(1)}, u32[32]{0:T(128)}, u32[]{:S(2)}) copy-start(u32[32]{0:T(128)} %constant.33) | copy-start | bytes 388
  0.0 13.5 %copy-start.2 = (s32[2]{0:T(128)S(1)}, s32[2]{0:T(128)}, u32[]{:S(2)}) copy-start(s32[2]{0:T(128)} %param.9) | copy-start | bytes 28
  0.0 26.5 %copy-start.1 = (f32[8]{0:T(128)S(1)}, f32[8]{0:T(128)}, u32[]{:S(2)}) copy-start(f32[8]{0:T(128)} %param.10) | copy-start | bytes 100
  4.8 21.8 %all-to-all-start = ((bf16[128,2,2,256]{3,2,1,0:T(2,128)(2,1)}), bf16[128,2,2,256]{3,2,1,0:T(2,128)(2,1)S(1)}, u32[]{:S(2)}, u32[]{:S(2)}) async-start(bf16[128,2,2,256]{3,2,1,0:T(2,128)(2,1)} %bitcast.2), calls=%async_computation | async-start | bytes 524288 | tf_op jit(solution)/shard_map/all_to_all | solution.py:168

commit v2 on v1

--- a/solution.py
+++ b/solution.py
@@ -3,6 +3,7 @@
 
 import jax
 import jax.numpy as jnp
+import numpy as np
 from jax import lax
 from jax.experimental import pallas as pl
 from jax.experimental.pallas import tpu as pltpu
@@ -69,20 +70,25 @@
             a_ref[kb * TILE + t] = rows[t]
 
 
-def filter_kernel(groups, imgs, coef_ref, bid_ref, kid_ref, noise_ref, out_ref, cf_ref, a_ref, c_ref, v_ref, d_ref):
-    q, width = coef_ref.shape
+def filter_kernel(groups, imgs, coef_ref, bid_ref, kid_ref, noise_ref, out_ref, *scratch):
+    coef = coef_ref[...].astype(jnp.float32)
+    done = filter_lanes(groups, imgs, coef, bid_ref[...], kid_ref[...], noise_ref[...], *scratch)
+    out_ref[...] = done.astype(jnp.bfloat16)
+
+
+def filter_lanes(groups, imgs, coef, bid, kid, noise, cf_ref, a_ref, c_ref, v_ref, d_ref):
+    q, width = coef.shape
     hq = q // 2
     slot = lax.broadcasted_iota(jnp.int32, (LANES, width), 0)
-    member = (slot % SLOTS == bid_ref[...]).astype(jnp.float32)
-    same = (slot % SLOTS // groups == kid_ref[...]).astype(jnp.float32)
+    member = (slot % SLOTS == bid).astype(jnp.float32)
+    same = (slot % SLOTS // groups == kid).astype(jnp.float32)
     low = slot < SLOTS
     weights = member + same * (prior_weight / imgs)
     w_lo = jnp.where(low, weights, 0.0).astype(jnp.bfloat16)
     w_hi = jnp.where(low, 0.0, weights).astype(jnp.bfloat16)
     counts = nt_dot(jnp.full((TILE, width), 0.5, jnp.bfloat16), member.astype(jnp.bfloat16))[0:1]
     scale = 1.0 / (counts + prior_weight)
-    noise = noise_ref[...]
-    cf_ref[...] = coef_ref[...].astype(jnp.float32)
+    cf_ref[...] = coef
     jj = lax.broadcasted_iota(jnp.int32, (hq, LANES), 0)
     col = jj + hq * (lax.broadcasted_iota(jnp.int32, (hq, LANES), 1) // SLOTS)
 
@@ -120,30 +126,217 @@
         return carry
 
     lax.fori_loop(0, q // TILE, apply, 0)
-    out_ref[...] = d_ref[...].astype(jnp.bfloat16)
+    return d_ref[...]
+
+
+def filter_scratch(q, width):
+    hq = q // 2
+    return [
+        pltpu.VMEM((q, width), jnp.float32),
+        pltpu.VMEM((q, hq, LANES), jnp.float32),
+        pltpu.VMEM((TILE, q, LANES), jnp.float32),
+        pltpu.VMEM((TILE, hq, LANES), jnp.float32),
+        pltpu.VMEM((q, width), jnp.float32),
+    ]
+
+
+VM = pl.BlockSpec(memory_space=pltpu.VMEM)
+PARAMS = pltpu.CompilerParams(vmem_limit_bytes=32 * 1024 * 1024)
 
 
 def wiener_filter(coef, bid, kid, noise, groups, imgs):
     q, width = coef.shape
-    hq = q // 2
     return pl.pallas_call(
         functools.partial(filter_kernel, groups, imgs),
         out_shape=jax.ShapeDtypeStruct((q, width), jnp.bfloat16),
-        in_specs=[pl.BlockSpec(memory_space=pltpu.VMEM)] * 4,
-        out_specs=pl.BlockSpec(memory_space=pltpu.VMEM),
-        scratch_shapes=[
-            pltpu.VMEM((q, width), jnp.float32),
-            pltpu.VMEM((q, hq, LANES), jnp.float32),
-            pltpu.VMEM((TILE, q, LANES), jnp.float32),
-            pltpu.VMEM((TILE, hq, LANES), jnp.float32),
-            pltpu.VMEM((q, width), jnp.float32),
-        ],
-        compiler_params=pltpu.CompilerParams(vmem_limit_bytes=32 * 1024 * 1024),
+        in_specs=[VM] * 4,
+        out_specs=VM,
+        scratch_shapes=filter_scratch(q, width),
+        compiler_params=PARAMS,
         name="wiener_filter",
     )(coef, bid, kid, noise)
 
 
+PACK = 4
+SHARE = 128 // PACK
+
+
+def lane_block(shape):
+    return lax.broadcasted_iota(jnp.int32, shape, 1) // SHARE
+
+
+def pack(tile):
+    step = tile.shape[0] // PACK
+    where = lane_block((step, 128))
+    blocks = []
+    for peer in range(PACK):
+        out = None
+        for j in range(PACK):
+            piece = tile[j * step:(j + 1) * step]
+            turn = (j - peer) * SHARE % 128
+            piece = pltpu.roll(piece, turn, 1) if turn else piece
+            out = piece if out is None else jnp.where(where == j, piece, out)
+        blocks.append(out)
+    return blocks
+
+
+def unpack(blocks):
+    step = blocks[0].shape[0]
+    where = lane_block((step, 128))
+    rows = []
+    for j in range(PACK):
+        out = None
+        for peer in range(PACK):
+            turn = (peer - j) * SHARE % 128
+            piece = pltpu.roll(blocks[peer], turn, 1) if turn else blocks[peer]
+            out = piece if out is None else jnp.where(where == peer, piece, out)
+        rows.append(out)
+    return jnp.concatenate(rows, axis=0)
+
+
+def project_kernel(per_shard, gid_ref, part_ref, table_ref, ctf_ref, white_ref, bessel_ref, out_ref, bess, sem):
+    images = part_ref.shape[0]
+    freqs, q, radii = bess.shape
+    shards = freqs // per_shard
+    fetch = pltpu.make_async_copy(bessel_ref, bess, sem)
+    fetch.start()
+    table = table_ref[...]
+    half = 2 * per_shard
+    spec = []
+    for i in range(images):
+        weight = ctf_ref[pl.ds(gid_ref[i], 1), :] * white_ref[...]
+        spec.append((nt_dot(table, part_ref[i]) * weight).astype(jnp.bfloat16))
+    lane = lax.broadcasted_iota(jnp.int32, (q, 128), 1)
+    lane_row = lax.broadcasted_iota(jnp.int32, (q // PACK, 128), 1) % SHARE // half
+    labels = jnp.zeros((q // PACK, 128), jnp.float32)
+    for i in range(images):
+        labels = jnp.where(lane_row == i, gid_ref[i].astype(jnp.float32), labels)
+    labels = labels.astype(jnp.bfloat16)
+    fetch.wait()
+    for t in range(shards // PACK):
+        rows = []
+        for peer in range(PACK):
+            d = t * PACK + peer
+            for i in range(images):
+                rows.append(spec[i][d * half:(d + 1) * half])
+        rows = jnp.concatenate(rows, axis=0)
+        acc = jnp.zeros((q, 128), jnp.float32)
+        for peer in range(PACK):
+            d = t * PACK + peer
+            block = bess[d * per_shard:(d + 1) * per_shard].reshape(per_shard * q, radii)
+            prod = nt_dot(block, rows)
+            for kk in range(per_shard):
+                here = (lane // SHARE == peer) & (lane % per_shard == kk)
+                acc = jnp.where(here, prod[kk * q:(kk + 1) * q], acc)
+        for peer, block in enumerate(pack(acc)):
+            d = t * PACK + peer
+            out_ref[d, 0:q // PACK] = block.astype(jnp.bfloat16)
+            out_ref[d, q // PACK:] = labels
+
+
+def packed_filter_kernel(groups, imgs, per_shard, in_ref, noise_ref, out_ref, *scratch):
+    shards, step = in_ref.shape[0], in_ref.shape[1] // 2
+    coef, ids = [], []
+    for t in range(shards // PACK):
+        blocks = [in_ref[t * PACK + peer].astype(jnp.float32) for peer in range(PACK)]
+        coef.append(unpack([block[:step] for block in blocks]))
+        row = blocks[0][step:step + 1]
+        for peer in range(1, PACK):
+            row = jnp.where(lane_block((1, 128)) == peer, blocks[peer][step:step + 1], row)
+        ids.append(row)
+    coef = jnp.concatenate(coef, axis=1)
+    ids = jnp.concatenate(ids, axis=1).astype(jnp.int32)
+    kid = lax.broadcasted_iota(jnp.int32, ids.shape, 1) % per_shard
+    done = filter_lanes(groups, imgs, coef, kid * groups + ids, kid, noise_ref[...], *scratch)
+    for t in range(shards // PACK):
+        for peer, block in enumerate(pack(done[:, t * 128:(t + 1) * 128])):
+            out_ref[t * PACK + peer] = block.astype(jnp.bfloat16)
+
+
+def restore_kernel(per_shard, in_ref, table_ref, bessel_ref, out_ref, bess, sem):
+    shards = in_ref.shape[0]
+    images = out_ref.shape[0]
+    q, radii = bess.shape[1:]
+    fetch = pltpu.make_async_copy(bessel_ref, bess, sem)
+    fetch.start()
+    half = 2 * per_shard
+    span = per_shard * q
+    keep = (
+        lax.broadcasted_iota(jnp.int32, (SHARE, span), 0) % per_shard
+        == lax.broadcasted_iota(jnp.int32, (SHARE, span), 1) // q
+    )
+    left = []
+    for t in range(shards // PACK):
+        tile = unpack([in_ref[t * PACK + peer].astype(jnp.float32) for peer in range(PACK)])
+        flat = jnp.transpose(tile)
+        for peer in range(PACK):
+            mine = flat[peer * SHARE:(peer + 1) * SHARE]
+            wide = jnp.concatenate([mine] * per_shard, axis=1)
+            left.append(jnp.where(keep, wide, 0.0).astype(jnp.bfloat16))
+    fetch.wait()
+    back = []
+    for d in range(shards):
+        block = bess[d * per_shard:(d + 1) * per_shard].reshape(span, radii)
+        back.append(jnp.dot(left[d], block, preferred_element_type=jnp.float32))
+    for i in range(images):
+        mine = jnp.concatenate([b[i * half:(i + 1) * half] for b in back], axis=0)
+        mine = jnp.transpose(mine).astype(jnp.bfloat16)
+        out_ref[i] = jnp.dot(mine, table_ref[...], preferred_element_type=jnp.float32).astype(jnp.bfloat16)
+
+
+def packed_body(particles, whitening, ctf, group_id, noise_var, bessel):
+    images, radii, angles = particles.shape
+    freqs, q = bessel.shape[:2]
+    groups = ctf.shape[0]
+    shards = lax.axis_size("img")
+    per_shard = freqs // shards
+    step = q // PACK
+    order = np.arange(freqs)[:, None] * np.arange(angles)[None, :] % angles
+    phase = 2.0 * math.pi / angles * order
+    table = np.stack([np.cos(phase), -np.sin(phase)], axis=0) / math.sqrt(angles)
+    table = table.reshape(2, shards, per_shard, angles).transpose(1, 0, 2, 3)
+    table = jnp.asarray(table.reshape(2 * freqs, angles), dtype=jnp.bfloat16)
+    whole = pl.BlockSpec(memory_space=pl.ANY)
+    sent = pl.pallas_call(
+        functools.partial(project_kernel, per_shard),
+        out_shape=jax.ShapeDtypeStruct((shards, 2 * step, 128), jnp.bfloat16),
+        in_specs=[pl.BlockSpec(memory_space=pltpu.SMEM), VM, VM, VM, VM, whole],
+        out_specs=VM,
+        scratch_shapes=[pltpu.VMEM(bessel.shape, jnp.bfloat16), pltpu.SemaphoreType.DMA],
+        compiler_params=PARAMS,
+        name="project",
+    )(group_id, particles, table, ctf, whitening[None, :], bessel)
+    arrived = lax.all_to_all(sent, "img", split_axis=0, concat_axis=0, tiled=True)
+    noise = jnp.tile(noise_var, LANES // groups)[None, :]
+    filtered = pl.pallas_call(
+        functools.partial(packed_filter_kernel, groups, shards * images, per_shard),
+        out_shape=jax.ShapeDtypeStruct((shards, step, 128), jnp.bfloat16),
+        in_specs=[VM, VM],
+        out_specs=VM,
+        scratch_shapes=filter_scratch(q, shards * SHARE),
+        compiler_params=PARAMS,
+        name="wiener_filter",
+    )(arrived, noise)
+    returned = lax.all_to_all(filtered, "img", split_axis=0, concat_axis=0, tiled=True)
+    return pl.pallas_call(
+        functools.partial(restore_kernel, per_shard),
+        out_shape=jax.ShapeDtypeStruct(particles.shape, jnp.bfloat16),
+        in_specs=[VM, VM, whole],
+        out_specs=VM,
+        scratch_shapes=[pltpu.VMEM(bessel.shape, jnp.bfloat16), pltpu.SemaphoreType.DMA],
+        compiler_params=PARAMS,
+        name="restore",
+    )(returned, table, bessel)
+
+
 def body(particles, whitening, ctf, group_id, noise_var, bessel):
+    share = 2 * particles.shape[0] * bessel.shape[0] // lax.axis_size("img")
+    if share == SHARE and bessel.shape[1] == SLOTS and lax.axis_size("img") % PACK == 0:
+        return packed_body(particles, whitening, ctf, group_id, noise_var, bessel)
+    return plain_body(particles, whitening, ctf, group_id, noise_var, bessel)
+
+
+def plain_body(particles, whitening, ctf, group_id, noise_var, bessel):
     img_count, radii, angles = particles.shape
     freqs, radial = bessel.shape[:2]
     groups = ctf.shape[0]

time: 61.7 us -> 56.8 us (0.921)
  blocking collectives: 25.1 us -> 9.48 us
  waiting for transfers between devices: 0.01 us -> 7.83 us
  Pallas kernels: 17.3 us -> 23.1 us
  local copies, waits for them, and re-layouts: 3.69 us -> 8.5 us
  matrix products: 4.64 us -> 0 us
  other arithmetic: 2.37 us -> 0 us
  between operations: 0.84 us -> 0.05 us
    unnamed x1 -> x0, blocking collectives: 12.4 us -> none
    all_to_all x1, waiting for transfers between devices: 0.01 us -> 7.83 us  [packed_body(): lax.all_to_all(sent, 'img', split_axis=0, concat_axis=0, tiled=True)]
    unnamed x11 -> x18, local copies, waits for them, and re-layouts: 0.85 us -> 8.42 us
    pallas_call x1 -> x3, Pallas kernels: 17.3 us -> 23.1 us  [the longest x1 17.3 us: packed_body(): pl.pallas_call(functools.partial(packed_filter_kernel, groups, shards * i...]
    dot_general x5 -> x0, matrix products: 4.64 us -> none  [the longest x1 1.18 us: body(): jnp.einsum('kqr,kipr->qkip', own_tables, arrived, preferred_element_type=...]
    all_to_all x1, blocking collectives: 12.6 us -> 9.48 us  [packed_body(): lax.all_to_all(filtered, 'img', split_axis=0, concat_axis=0, tiled=True)]
    convert_element_type x1 -> x0, other arithmetic: 1.22 us -> none  [body(): (particles.astype(jnp.float32) * weight_rows[:, :, None]).astype(jnp.bflo...]
    reshape x3 -> x0, local copies, waits for them, and re-layouts: 1.14 us -> none  [the longest x2 1.05 us: body(): spectrum = spectrum.astype(jnp.bfloat16).reshape(img_count, radii, 2, freqs)]
  transfers between devices with their start and end apart: 1 -> 1, of which waited for: 0 -> 1; matrix products, arithmetic and copies ran while one was open for 2% -> 0% of each run, Pallas kernels for 0% -> 0%
where the time goes in v2:
time: 56.8 us; the launch traced here: 56.3 us
  Pallas kernels  23.1 us (41%)
  blocking collectives  9.48 us (17%)
  local copies, waits for them, and re-layouts  8.5 us (15%)
  waiting for transfers between devices  7.83 us (14%)
  starting transfers between devices  7.4 us (13%)
    pallas_call x1, Pallas kernels, packed_body(): pl.pallas_call(functools.partial(packed_filter_kernel, groups, shards * i...  17.3 us
    all_to_all x1, blocking collectives, packed_body(): lax.all_to_all(filtered, 'img', split_axis=0, concat_axis=0, tiled=True)  9.48 us
    unnamed x18, local copies, waits for them, and re-layouts  8.42 us
    all_to_all x1, waiting for transfers between devices, packed_body(): lax.all_to_all(sent, 'img', split_axis=0, concat_axis=0, tiled=True)  7.83 us
    all_to_all x1, starting transfers between devices, packed_body(): lax.all_to_all(sent, 'img', split_axis=0, concat_axis=0, tiled=True)  7.4 us
    pallas_call x1, Pallas kernels, packed_body(): pl.pallas_call(functools.partial(project_kernel, per_shard), out_shape=ja...  3.14 us
    pallas_call x1, Pallas kernels, packed_body(): pl.pallas_call(functools.partial(restore_kernel, per_shard), out_shape=ja...  2.66 us
  transfers between devices with their start and end apart: 1, of which 1 were waited for; matrix products, arithmetic and copies ran while one was open for 0% of the time, Pallas kernels for 0%

profile of v2, /device:TPU:0, one launch (start us, length us, event | category | flops | bytes accessed | tf_op | source)
XLA Modules:
  0.0 56.3 jit_solution(13976313075351827912)
XLA Ops:
  0.0 0.0 copy-start.8
  0.0 2.2 %copy-done = bf16[128,64,256]{2,1,0:T(8,128)(2,1)S(1)} copy-done((bf16[128,64,256]{2,1,0:T(8,128)(2,1)S(1)}, bf16[128,64,256]{2,1,0:T(8,128)(2,1)}, u32[]{:S(2)}) %copy-start) | copy-done | bytes 4194328
  2.2 0.0 copy-start.2
  2.2 0.9 %copy-done.2 = bf16[256,512]{1,0:T(8,128)(2,1)S(1)} copy-done((bf16[256,512]{1,0:T(8,128)(2,1)S(1)}, bf16[256,512]{1,0:T(8,128)(2,1)}, u32[]{:S(2)}) %copy-start.2) | copy-done | bytes 262168
  3.2 0.0 copy-start.4
  3.2 1.0 %copy-done.4 = bf16[2,256,512]{2,1,0:T(8,128)(2,1)S(1)} copy-done((bf16[2,256,512]{2,1,0:T(8,128)(2,1)S(1)}, bf16[2,256,512]{2,1,0:T(8,128)(2,1)}, u32[]{:S(2)}) %copy-start.4) | copy-done | bytes 524312
  4.2 0.0 copy-start.5
  4.2 0.7 %copy-done.5 = f32[8,256]{1,0:T(8,128)S(1)} copy-done((f32[8,256]{1,0:T(8,128)S(1)}, f32[8,256]{1,0:T(8,128)}, u32[]{:S(2)}) %copy-start.5) | copy-done | bytes 8216
  4.9 0.0 copy-start.6
  4.9 0.7 %copy-done.6 = f32[256]{0:T(256)S(1)} copy-done((f32[256]{0:T(256)S(1)}, f32[256]{0:T(256)}, u32[]{:S(2)}) %copy-start.6) | copy-done | bytes 1048
  5.6 0.0 copy-start.7
  5.6 0.7 %copy-done.7 = s32[2]{0:T(128)S(1)} copy-done((s32[2]{0:T(128)S(1)}, s32[2]{0:T(128)}, u32[]{:S(2)}) %copy-start.7) | copy-done | bytes 32
  6.2 0.0 copy-start.3
  6.2 3.1 %project.1 = bf16[16,32,128]{2,1,0:T(8,128)(2,1)} custom-call(s32[2]{0:T(128)S(1)} %copy-done.7, bf16[2,256,512]{2,1,0:T(8,128)(2,1)S(1)} %copy-done.4, bf16[256,512]{1,0:T(8,128)(2,1)S(1)} %copy-done.2, f32[8,256]{1,0:T(8,128)S(1)} %copy-done.5, f32[1,256]{1,0:T(1,128)S(1)} %bitcast.1, bf16[128,64,256]{2,1,0:T(8,128)(2,1)S(1)} %copy-done), custom_call_target="tpu_custom_call" | custom-call | tf_op jit(solution)/shard_map/project/pallas_call | solution.py:300
  9.4 7.4 %all-to-all-start = ((bf16[16,32,128]{2,1,0:T(8,128)(2,1)}), bf16[16,32,128]{2,1,0:T(8,128)(2,1)S(1)}, u32[]{:S(2)}, u32[]{:S(2)}) async-start(bf16[16,32,128]{2,1,0:T(8,128)(2,1)} %project.1), calls=%async_computation | async-start | bytes 262144 | tf_op jit(solution)/shard_map/all_to_all | solution.py:309
  16.8 0.0 copy-done.8
  16.8 0.1 broadcast_in_dim_tile.3.noise_ref
  16.9 7.8 %all-to-all-done.in_ref = bf16[16,32,128]{2,1,0:T(8,128)(2,1)S(1)} async-done(((bf16[16,32,128]{2,1,0:T(8,128)(2,1)}), bf16[16,32,128]{2,1,0:T(8,128)(2,1)S(1)}, u32[]{:S(2)}, u32[]{:S(2)}) %all-to-all-start) | async-done | bytes 131104 | tf_op jit(solution)/shard_map/all_to_all | solution.py:309
  24.7 17.3 %wiener_filter.1 = bf16[16,16,128]{2,1,0:T(8,128)(2,1)S(1)} custom-call(bf16[16,32,128]{2,1,0:T(8,128)(2,1)S(1)} %all-to-all-done.in_ref, f32[1,128]{1,0:T(1,128)S(1)} %broadcast_in_dim_tile.3.noise_ref), custom_call_target="tpu_custom_call" | custom-call | tf_op jit(solution)/shard_map/wiener_filter/pallas_call | solution.py:311
  42.0 9.5 %all_to_all.10.in_ref = bf16[16,16,128]{2,1,0:T(8,128)(2,1)S(1)} all-to-all(bf16[16,16,128]{2,1,0:T(8,128)(2,1)S(1)} %wiener_filter.1), channel_id=1, replica_groups=mesh['grp'=2,'img'=16] {'img'}, dimensions={0} | all-to-all | bytes 131072 | tf_op jit(solution)/shard_map/all_to_all | solution.py:320
  51.5 0.0 copy-done.3
  51.5 0.0 copy-start.1
  51.5 2.2 %copy-done.1 = bf16[128,64,256]{2,1,0:T(8,128)(2,1)S(1)} copy-done((bf16[128,64,256]{2,1,0:T(8,128)(2,1)S(1)}, bf16[128,64,256]{2,1,0:T(8,128)(2,1)}, u32[]{:S(2)}) %copy-start.1) | copy-done | bytes 4194328
  53.7 2.7 %restore.1 = bf16[2,256,512]{2,1,0:T(8,128)(2,1)} custom-call(bf16[16,16,128]{2,1,0:T(8,128)(2,1)S(1)} %all_to_all.10.in_ref, bf16[256,512]{1,0:T(8,128)(2,1)S(1)} %copy-done.3, bf16[128,64,256]{2,1,0:T(8,128)(2,1)S(1)} %copy-done.1), custom_call_target="tpu_custom_call" | custom-call | tf_op jit(solution)/shard_map/restore/pallas_call | solution.py:321
  (2 shorter events, 0.0 us)
Async XLA Ops:
  0.0 16.8 %copy-start.8 = (f32[8]{0:T(128)S(1)}, f32[8]{0:T(128)}, u32[]{:S(2)}) copy-start(f32[8]{0:T(128)} %param.11) | copy-start | bytes 100
  0.0 2.2 %copy-start = (bf16[128,64,256]{2,1,0:T(8,128)(2,1)S(1)}, bf16[128,64,256]{2,1,0:T(8,128)(2,1)}, u32[]{:S(2)}) copy-start(bf16[128,64,256]{2,1,0:T(8,128)(2,1)} %bessel_ref.3) | copy-start | bytes 12582916
  2.2 0.9 %copy-start.2 = (bf16[256,512]{1,0:T(8,128)(2,1)S(1)}, bf16[256,512]{1,0:T(8,128)(2,1)}, u32[]{:S(2)}) copy-start(bf16[256,512]{1,0:T(8,128)(2,1)} %constant.2.clone.table_ref) | copy-start | bytes 786436
  3.2 1.0 %copy-start.4 = (bf16[2,256,512]{2,1,0:T(8,128)(2,1)S(1)}, bf16[2,256,512]{2,1,0:T(8,128)(2,1)}, u32[]{:S(2)}) copy-start(bf16[2,256,512]{2,1,0:T(8,128)(2,1)} %part_ref.1) | copy-start | bytes 1572868
  4.2 0.7 %copy-start.5 = (f32[8,256]{1,0:T(8,128)S(1)}, f32[8,256]{1,0:T(8,128)}, u32[]{:S(2)}) copy-start(f32[8,256]{1,0:T(8,128)} %ctf_ref.1) | copy-start | bytes 24580
  4.9 0.7 %copy-start.6 = (f32[256]{0:T(256)S(1)}, f32[256]{0:T(256)}, u32[]{:S(2)}) copy-start(f32[256]{0:T(256)} %param.8) | copy-start | bytes 3076
  5.6 0.7 %copy-start.7 = (s32[2]{0:T(128)S(1)}, s32[2]{0:T(128)}, u32[]{:S(2)}) copy-start(s32[2]{0:T(128)} %gid_ref.1) | copy-start | bytes 28
  6.2 45.3 %copy-start.3 = (bf16[256,512]{1,0:T(8,128)(2,1)S(1)}, bf16[256,512]{1,0:T(8,128)(2,1)}, u32[]{:S(2)}) copy-start(bf16[256,512]{1,0:T(8,128)(2,1)} %constant.2.clone.table_ref) | copy-start | bytes 786436
  9.4 15.3 %all-to-all-start = ((bf16[16,32,128]{2,1,0:T(8,128)(2,1)}), bf16[16,32,128]{2,1,0:T(8,128)(2,1)S(1)}, u32[]{:S(2)}, u32[]{:S(2)}) async-start(bf16[16,32,128]{2,1,0:T(8,128)(2,1)} %project.1), calls=%async_computation | async-start | bytes 262144 | tf_op jit(solution)/shard_map/all_to_all | solution.py:309
  51.5 2.2 %copy-start.1 = (bf16[128,64,256]{2,1,0:T(8,128)(2,1)S(1)}, bf16[128,64,256]{2,1,0:T(8,128)(2,1)}, u32[]{:S(2)}) copy-start(bf16[128,64,256]{2,1,0:T(8,128)(2,1)} %bessel_ref.3) | copy-start | bytes 12582916

commit v3 on v2

--- a/solution.py
+++ b/solution.py
@@ -194,25 +194,76 @@
     return jnp.concatenate(rows, axis=0)
 
 
-def project_kernel(per_shard, gid_ref, part_ref, table_ref, ctf_ref, white_ref, bessel_ref, out_ref, bess, sem):
+def greet(shards, me):
+    barrier = pltpu.get_barrier_semaphore()
+    for d in range(shards):
+        @pl.when(d != me)
+        def _():
+            pl.semaphore_signal(
+                barrier, inc=1, device_id={"img": d}, device_id_type=pl.DeviceIdType.MESH
+            )
+    pl.semaphore_wait(barrier, shards - 1)
+
+
+def to_peer(src_ref, dst_ref, d, me, send_sem, recv_sem):
+    return pltpu.make_async_remote_copy(
+        src_ref=src_ref.at[d],
+        dst_ref=dst_ref.at[me],
+        send_sem=send_sem.at[d],
+        recv_sem=recv_sem.at[me],
+        device_id={"img": d},
+        device_id_type=pl.DeviceIdType.MESH,
+    )
+
+
+def from_peer(src_ref, dst_ref, d, send_sem, recv_sem):
+    return pltpu.make_async_remote_copy(
+        src_ref=src_ref.at[d],
+        dst_ref=dst_ref.at[d],
+        send_sem=send_sem.at[d],
+        recv_sem=recv_sem.at[d],
+        device_id={"img": d},
+        device_id_type=pl.DeviceIdType.MESH,
+    )
+
+
+def project_kernel(
+    per_shard, gid_ref, part_hbm, table_hbm, ctf_hbm, white_hbm, bessel_hbm, out_ref,
+    part_ref, table_ref, ctf_ref, white_ref, bess, sent, sem, send_sem, recv_sem,
+):
     images = part_ref.shape[0]
     freqs, q, radii = bess.shape
     shards = freqs // per_shard
-    fetch = pltpu.make_async_copy(bessel_ref, bess, sem)
-    fetch.start()
+    me = lax.axis_index("img")
+    loads = [
+        pltpu.make_async_copy(src, dst, sem.at[n])
+        for n, (src, dst) in enumerate((
+            (ctf_hbm, ctf_ref), (white_hbm, white_ref), (table_hbm, table_ref),
+            (part_hbm, part_ref), (bessel_hbm, bess),
+        ))
+    ]
+    for load in loads:
+        load.start()
+    greet(shards, me)
+    half = 2 * per_shard
+    step = q // PACK
+    lane = lax.broadcasted_iota(jnp.int32, (q, 128), 1)
+    lane_row = lax.broadcasted_iota(jnp.int32, (step, 128), 1) % SHARE // half
+    labels = jnp.zeros((step, 128), jnp.float32)
+    for i in range(images):
+        labels = jnp.where(lane_row == i, gid_ref[i].astype(jnp.float32), labels)
+    labels = labels.astype(jnp.bfloat16)
+    for load in loads[:4]:
+        load.wait()
     table = table_ref[...]
-    half = 2 * per_shard
     spec = []
     for i in range(images):
         weight = ctf_ref[pl.ds(gid_ref[i], 1), :] * white_ref[...]
-        spec.append((nt_dot(table, part_ref[i]) * weight).astype(jnp.bfloat16))
-    lane = lax.broadcasted_iota(jnp.int32, (q, 128), 1)
-    lane_row = lax.broadcasted_iota(jnp.int32, (q // PACK, 128), 1) % SHARE // half
-    labels = jnp.zeros((q // PACK, 128), jnp.float32)
-    for i in range(images):
-        labels = jnp.where(lane_row == i, gid_ref[i].astype(jnp.float32), labels)
-    labels = labels.astype(jnp.bfloat16)
-    fetch.wait()
+        weight = jnp.transpose(jnp.broadcast_to(weight, (128, radii)))
+        weight = jnp.concatenate([weight] * (part_ref.shape[2] // 128), axis=1)
+        filtered = (part_ref[i].astype(jnp.float32) * weight).astype(jnp.bfloat16)
+        spec.append(nt_dot(table, filtered).astype(jnp.bfloat16))
+    loads[4].wait()
     for t in range(shards // PACK):
         rows = []
         for peer in range(PACK):
@@ -230,8 +281,18 @@
                 acc = jnp.where(here, prod[kk * q:(kk + 1) * q], acc)
         for peer, block in enumerate(pack(acc)):
             d = t * PACK + peer
-            out_ref[d, 0:q // PACK] = block.astype(jnp.bfloat16)
-            out_ref[d, q // PACK:] = labels
+            sent[d, 0:step] = block.astype(jnp.bfloat16)
+            sent[d, step:2 * step] = labels
+
+            @pl.when(d != me)
+            def _():
+                to_peer(sent, out_ref, d, me, send_sem, recv_sem).start()
+
+    out_ref[me] = sent[me]
+    for d in range(shards):
+        @pl.when(d != me)
+        def _():
+            from_peer(sent, out_ref, d, send_sem, recv_sem).wait()
 
 
 def packed_filter_kernel(groups, imgs, per_shard, in_ref, noise_ref, out_ref, *scratch):
@@ -247,41 +308,74 @@
     coef = jnp.concatenate(coef, axis=1)
     ids = jnp.concatenate(ids, axis=1).astype(jnp.int32)
     kid = lax.broadcasted_iota(jnp.int32, ids.shape, 1) % per_shard
-    done = filter_lanes(groups, imgs, coef, kid * groups + ids, kid, noise_ref[...], *scratch)
+    group = lax.broadcasted_iota(jnp.int32, (1, LANES), 1) % groups
+    noise = jnp.zeros((1, LANES), jnp.float32)
+    for g in range(groups):
+        noise = jnp.where(group == g, noise_ref[g], noise)
+    done = filter_lanes(groups, imgs, coef, kid * groups + ids, kid, noise, *scratch)
     for t in range(shards // PACK):
         for peer, block in enumerate(pack(done[:, t * 128:(t + 1) * 128])):
             out_ref[t * PACK + peer] = block.astype(jnp.bfloat16)
 
 
-def restore_kernel(per_shard, in_ref, table_ref, bessel_ref, out_ref, bess, sem):
+def restore_kernel(
+    per_shard, in_ref, table_hbm, bessel_hbm, out_hbm,
+    table_ref, bess, out_ref, held, sem, out_sem, send_sem, recv_sem,
+):
     shards = in_ref.shape[0]
     images = out_ref.shape[0]
     q, radii = bess.shape[1:]
-    fetch = pltpu.make_async_copy(bessel_ref, bess, sem)
-    fetch.start()
+    me = lax.axis_index("img")
+    loads = [
+        pltpu.make_async_copy(table_hbm, table_ref, sem.at[0]),
+        pltpu.make_async_copy(bessel_hbm, bess, sem.at[1]),
+    ]
+    for load in loads:
+        load.start()
+    greet(shards, me)
+    for d in range(shards):
+        @pl.when(d != me)
+        def _():
+            to_peer(in_ref, held, d, me, send_sem, recv_sem).start()
+    held[me] = in_ref[me]
     half = 2 * per_shard
     span = per_shard * q
     keep = (
         lax.broadcasted_iota(jnp.int32, (SHARE, span), 0) % per_shard
         == lax.broadcasted_iota(jnp.int32, (SHARE, span), 1) // q
     )
-    left = []
+    for load in loads:
+        load.wait()
+    for d in range(shards):
+        @pl.when(d != me)
+        def _():
+            from_peer(in_ref, held, d, send_sem, recv_sem).wait()
+    back = []
     for t in range(shards // PACK):
-        tile = unpack([in_ref[t * PACK + peer].astype(jnp.float32) for peer in range(PACK)])
+        tile = unpack([held[t * PACK + peer].astype(jnp.float32) for peer in range(PACK)])
         flat = jnp.transpose(tile)
         for peer in range(PACK):
+            d = t * PACK + peer
             mine = flat[peer * SHARE:(peer + 1) * SHARE]
             wide = jnp.concatenate([mine] * per_shard, axis=1)
-            left.append(jnp.where(keep, wide, 0.0).astype(jnp.bfloat16))
-    fetch.wait()
-    back = []
-    for d in range(shards):
-        block = bess[d * per_shard:(d + 1) * per_shard].reshape(span, radii)
-        back.append(jnp.dot(left[d], block, preferred_element_type=jnp.float32))
+            left = jnp.where(keep, wide, 0.0).astype(jnp.bfloat16)
+            block = bess[d * per_shard:(d + 1) * per_shard].reshape(span, radii)
+            back.append(jnp.dot(left, block, preferred_element_type=jnp.float32))
+    stores = []
     for i in range(images):
         mine = jnp.concatenate([b[i * half:(i + 1) * half] for b in back], axis=0)
         mine = jnp.transpose(mine).astype(jnp.bfloat16)
         out_ref[i] = jnp.dot(mine, table_ref[...], preferred_element_type=jnp.float32).astype(jnp.bfloat16)
+        stores.append(pltpu.make_async_copy(out_ref.at[i], out_hbm.at[i], out_sem.at[i]))
+        stores[i].start()
+    for store in stores:
+        store.wait()
+
+
+def remote_params(n):
+    return pltpu.CompilerParams(
+        vmem_limit_bytes=32 * 1024 * 1024, collective_id=n, has_side_effects=True
+    )
 
 
 def packed_body(particles, whitening, ctf, group_id, noise_var, bessel):
@@ -296,37 +390,54 @@
     table = np.stack([np.cos(phase), -np.sin(phase)], axis=0) / math.sqrt(angles)
     table = table.reshape(2, shards, per_shard, angles).transpose(1, 0, 2, 3)
     table = jnp.asarray(table.reshape(2 * freqs, angles), dtype=jnp.bfloat16)
-    whole = pl.BlockSpec(memory_space=pl.ANY)
-    sent = pl.pallas_call(
+    hbm = pl.BlockSpec(memory_space=pltpu.HBM)
+    smem = pl.BlockSpec(memory_space=pltpu.SMEM)
+    arrived = pl.pallas_call(
         functools.partial(project_kernel, per_shard),
         out_shape=jax.ShapeDtypeStruct((shards, 2 * step, 128), jnp.bfloat16),
-        in_specs=[pl.BlockSpec(memory_space=pltpu.SMEM), VM, VM, VM, VM, whole],
+        in_specs=[smem, hbm, hbm, hbm, hbm, hbm],
         out_specs=VM,
-        scratch_shapes=[pltpu.VMEM(bessel.shape, jnp.bfloat16), pltpu.SemaphoreType.DMA],
-        compiler_params=PARAMS,
+        scratch_shapes=[
+            pltpu.VMEM(particles.shape, jnp.bfloat16),
+            pltpu.VMEM(table.shape, jnp.bfloat16),
+            pltpu.VMEM(ctf.shape, jnp.float32),
+            pltpu.VMEM((1, radii), jnp.float32),
+            pltpu.VMEM(bessel.shape, jnp.bfloat16),
+            pltpu.VMEM((shards, 2 * step, 128), jnp.bfloat16),
+            pltpu.SemaphoreType.DMA((5,)),
+            pltpu.SemaphoreType.DMA((shards,)),
+            pltpu.SemaphoreType.DMA((shards,)),
+        ],
+        compiler_params=remote_params(0),
         name="project",
     )(group_id, particles, table, ctf, whitening[None, :], bessel)
-    arrived = lax.all_to_all(sent, "img", split_axis=0, concat_axis=0, tiled=True)
-    noise = jnp.tile(noise_var, LANES // groups)[None, :]
     filtered = pl.pallas_call(
         functools.partial(packed_filter_kernel, groups, shards * images, per_shard),
         out_shape=jax.ShapeDtypeStruct((shards, step, 128), jnp.bfloat16),
-        in_specs=[VM, VM],
+        in_specs=[VM, smem],
         out_specs=VM,
         scratch_shapes=filter_scratch(q, shards * SHARE),
         compiler_params=PARAMS,
         name="wiener_filter",
-    )(arrived, noise)
-    returned = lax.all_to_all(filtered, "img", split_axis=0, concat_axis=0, tiled=True)
+    )(arrived, noise_var)
     return pl.pallas_call(
         functools.partial(restore_kernel, per_shard),
         out_shape=jax.ShapeDtypeStruct(particles.shape, jnp.bfloat16),
-        in_specs=[VM, VM, whole],
-        out_specs=VM,
-        scratch_shapes=[pltpu.VMEM(bessel.shape, jnp.bfloat16), pltpu.SemaphoreType.DMA],
-        compiler_params=PARAMS,
+        in_specs=[VM, hbm, hbm],
+        out_specs=hbm,
+        scratch_shapes=[
+            pltpu.VMEM(table.shape, jnp.bfloat16),
+            pltpu.VMEM(bessel.shape, jnp.bfloat16),
+            pltpu.VMEM(particles.shape, jnp.bfloat16),
+            pltpu.VMEM((shards, step, 128), jnp.bfloat16),
+            pltpu.SemaphoreType.DMA((2,)),
+            pltpu.SemaphoreType.DMA((images,)),
+            pltpu.SemaphoreType.DMA((shards,)),
+            pltpu.SemaphoreType.DMA((shards,)),
+        ],
+        compiler_params=remote_params(1),
         name="restore",
-    )(returned, table, bessel)
+    )(filtered, table, bessel)
 
 
 def body(particles, whitening, ctf, group_id, noise_var, bessel):

time: 56.8 us -> 47 us (0.83)
  Pallas kernels: 23.1 us -> 39.7 us
  blocking collectives: 9.48 us -> 0 us
  waiting for transfers between devices: 7.83 us -> 0 us
  starting transfers between devices: 7.4 us -> 0 us
  local copies, waits for them, and re-layouts: 8.5 us -> 7.02 us
    all_to_all x1 -> x0, blocking collectives: 9.48 us -> none  [packed_body(): lax.all_to_all(filtered, 'img', split_axis=0, concat_axis=0, tiled=True)]
    pallas_call x1, Pallas kernels: 3.14 us -> 11.5 us  [packed_body(): pl.pallas_call(functools.partial(project_kernel, per_shard), out_shape=ja...]
    all_to_all x1 -> x0, waiting for transfers between devices: 7.83 us -> none  [packed_body(): lax.all_to_all(sent, 'img', split_axis=0, concat_axis=0, tiled=True)]
    pallas_call x1, Pallas kernels: 2.66 us -> 10.4 us  [packed_body(): pl.pallas_call(functools.partial(restore_kernel, per_shard), out_shape=ja...]
    all_to_all x1 -> x0, starting transfers between devices: 7.4 us -> none  [packed_body(): lax.all_to_all(sent, 'img', split_axis=0, concat_axis=0, tiled=True)]
    unnamed x18 -> x17, local copies, waits for them, and re-layouts: 8.42 us -> 7.02 us
    pallas_call x1, Pallas kernels: 17.3 us -> 17.8 us  [packed_body(): pl.pallas_call(functools.partial(packed_filter_kernel, groups, shards * i...]
  transfers between devices with their start and end apart: 1 -> 0, of which waited for: 1 -> 0; matrix products, arithmetic and copies ran while one was open for 0% -> 0% of each run, Pallas kernels for 0% -> 0%
where the time goes in v3:
time: 47 us; the launch traced here: 46.7 us
  Pallas kernels  39.7 us (84%)
  local copies, waits for them, and re-layouts  7.02 us (15%)
    pallas_call x1, Pallas kernels, packed_body(): pl.pallas_call(functools.partial(packed_filter_kernel, groups, shards * i...  17.8 us
    pallas_call x1, Pallas kernels, packed_body(): pl.pallas_call(functools.partial(project_kernel, per_shard), out_shape=ja...  11.5 us
    pallas_call x1, Pallas kernels, packed_body(): pl.pallas_call(functools.partial(restore_kernel, per_shard), out_shape=ja...  10.4 us
    unnamed x17, local copies, waits for them, and re-layouts  7.02 us

profile of v3, /device:TPU:0, one launch (start us, length us, event | category | flops | bytes accessed | tf_op | source)
XLA Modules:
  0.0 46.7 jit_solution(9898038886063931083)
XLA Ops:
  0.0 0.0 copy-start.7
  0.0 0.0 copy-start
  0.0 2.2 %copy-done = bf16[128,64,256]{2,1,0:T(8,128)(2,1)S(1)} copy-done((bf16[128,64,256]{2,1,0:T(8,128)(2,1)S(1)}, bf16[128,64,256]{2,1,0:T(8,128)(2,1)}, u32[]{:S(2)}) %copy-start) | copy-done | bytes 4194328
  2.2 0.0 copy-start.2
  2.2 0.9 %copy-done.2 = bf16[256,512]{1,0:T(8,128)(2,1)S(1)} copy-done((bf16[256,512]{1,0:T(8,128)(2,1)S(1)}, bf16[256,512]{1,0:T(8,128)(2,1)}, u32[]{:S(2)}) %copy-start.2) | copy-done | bytes 262168
  3.2 0.0 copy-start.3
  3.2 1.0 %copy-done.3 = bf16[2,256,512]{2,1,0:T(8,128)(2,1)S(1)} copy-done((bf16[2,256,512]{2,1,0:T(8,128)(2,1)S(1)}, bf16[2,256,512]{2,1,0:T(8,128)(2,1)}, u32[]{:S(2)}) %copy-start.3) | copy-done | bytes 524312
  4.2 0.0 copy-start.4
  4.2 0.7 %copy-done.4 = f32[8,256]{1,0:T(8,128)S(1)} copy-done((f32[8,256]{1,0:T(8,128)S(1)}, f32[8,256]{1,0:T(8,128)}, u32[]{:S(2)}) %copy-start.4) | copy-done | bytes 8216
  4.9 0.0 copy-start.5
  4.9 0.7 %copy-done.5 = f32[256]{0:T(256)S(1)} copy-done((f32[256]{0:T(256)S(1)}, f32[256]{0:T(256)}, u32[]{:S(2)}) %copy-start.5) | copy-done | bytes 1048
  5.6 0.0 copy-start.6
  5.6 0.7 %copy-done.6 = s32[2]{0:T(128)S(1)} copy-done((s32[2]{0:T(128)S(1)}, s32[2]{0:T(128)}, u32[]{:S(2)}) %copy-start.6) | copy-done | bytes 32
  6.2 0.0 copy-start.1
  6.2 11.5 %project.1.in_ref = bf16[16,32,128]{2,1,0:T(8,128)(2,1)S(1)} custom-call(s32[2]{0:T(128)S(1)} %copy-done.6, bf16[2,256,512]{2,1,0:T(8,128)(2,1)S(1)} %copy-done.3, bf16[256,512]{1,0:T(8,128)(2,1)S(1)} %copy-done.2, f32[8,256]{1,0:T(8,128)S(1)} %copy-done.4, f32[1,256]{1,0:T(1,128)S(1)} %bitcast.1, bf16[128,64,256]{2,1,0:T(8,128)(2,1)S(1)} %copy-done), custom_call_target="tpu_custom_call" | custom-call | tf_op jit(solution)/shard_map/project/pallas_call | solution.py:395
  17.7 0.0 copy-done.7
  17.7 17.8 %wiener_filter.1.in_ref = bf16[16,16,128]{2,1,0:T(8,128)(2,1)S(1)} custom-call(bf16[16,32,128]{2,1,0:T(8,128)(2,1)S(1)} %project.1.in_ref, f32[8]{0:T(128)S(1)} %copy-done.7), custom_call_target="tpu_custom_call" | custom-call | tf_op jit(solution)/shard_map/wiener_filter/pallas_call | solution.py:414
  35.6 0.0 copy-done.1
  35.6 10.4 %restore.1 = bf16[2,256,512]{2,1,0:T(8,128)(2,1)S(1)} custom-call(bf16[16,16,128]{2,1,0:T(8,128)(2,1)S(1)} %wiener_filter.1.in_ref, bf16[256,512]{1,0:T(8,128)(2,1)S(1)} %copy-done.2, bf16[128,64,256]{2,1,0:T(8,128)(2,1)S(1)} %copy-done.1), custom_call_target="tpu_custom_call" | custom-call | tf_op jit(solution)/shard_map/restore/pallas_call | solution.py:423
  45.9 0.8 %copy.9 = bf16[2,256,512]{2,1,0:T(8,128)(2,1)} copy(bf16[2,256,512]{2,1,0:T(8,128)(2,1)S(1)} %restore.1) | data formatting | bytes 1048576
Async XLA Ops:
  0.0 17.7 %copy-start.7 = (f32[8]{0:T(128)S(1)}, f32[8]{0:T(128)}, u32[]{:S(2)}) copy-start(f32[8]{0:T(128)} %noise_ref.1) | copy-start | bytes 100
  0.0 2.2 %copy-start = (bf16[128,64,256]{2,1,0:T(8,128)(2,1)S(1)}, bf16[128,64,256]{2,1,0:T(8,128)(2,1)}, u32[]{:S(2)}) copy-start(bf16[128,64,256]{2,1,0:T(8,128)(2,1)} %bessel_hbm.3) | copy-start | bytes 12582916
  2.2 0.9 %copy-start.2 = (bf16[256,512]{1,0:T(8,128)(2,1)S(1)}, bf16[256,512]{1,0:T(8,128)(2,1)}, u32[]{:S(2)}) copy-start(bf16[256,512]{1,0:T(8,128)(2,1)} %constant.2.clone.table_hbm) | copy-start | bytes 786436
  3.2 1.0 %copy-start.3 = (bf16[2,256,512]{2,1,0:T(8,128)(2,1)S(1)}, bf16[2,256,512]{2,1,0:T(8,128)(2,1)}, u32[]{:S(2)}) copy-start(bf16[2,256,512]{2,1,0:T(8,128)(2,1)} %part_hbm.1) | copy-start | bytes 1572868
  4.2 0.7 %copy-start.4 = (f32[8,256]{1,0:T(8,128)S(1)}, f32[8,256]{1,0:T(8,128)}, u32[]{:S(2)}) copy-start(f32[8,256]{1,0:T(8,128)} %ctf_hbm.1) | copy-start | bytes 24580
  4.9 0.7 %copy-start.5 = (f32[256]{0:T(256)S(1)}, f32[256]{0:T(256)}, u32[]{:S(2)}) copy-start(f32[256]{0:T(256)} %param.8) | copy-start | bytes 3076
  5.6 0.7 %copy-start.6 = (s32[2]{0:T(128)S(1)}, s32[2]{0:T(128)}, u32[]{:S(2)}) copy-start(s32[2]{0:T(128)} %gid_ref.1) | copy-start | bytes 28
  6.2 29.3 %copy-start.1 = (bf16[128,64,256]{2,1,0:T(8,128)(2,1)S(1)}, bf16[128,64,256]{2,1,0:T(8,128)(2,1)}, u32[]{:S(2)}) copy-start(bf16[128,64,256]{2,1,0:T(8,128)(2,1)} %bessel_hbm.3) | copy-start | bytes 12582916

commit v4 on v3

--- a/solution.py
+++ b/solution.py
@@ -13,6 +13,7 @@
 SLOTS = 64
 LANES = 2 * SLOTS
 TILE = 8
+VMEM_LIMIT = 60 * 1024 * 1024
 
 
 def angle_table(angles, freqs):
@@ -227,9 +228,10 @@
     )
 
 
-def project_kernel(
-    per_shard, gid_ref, part_hbm, table_hbm, ctf_hbm, white_hbm, bessel_hbm, out_ref,
-    part_ref, table_ref, ctf_ref, white_ref, bess, sent, sem, send_sem, recv_sem,
+def fused_kernel(
+    per_shard, groups, gid_ref, noise_ref, part_hbm, table_hbm, ctf_hbm, white_hbm, bessel_hbm, out_hbm,
+    part_ref, table_ref, ctf_ref, white_ref, bess, sent, came, answer, held, out_ref,
+    sem, out_sem, send_sem, recv_sem, send_sem2, recv_sem2, *scratch,
 ):
     images = part_ref.shape[0]
     freqs, q, radii = bess.shape
@@ -286,20 +288,17 @@
 
             @pl.when(d != me)
             def _():
-                to_peer(sent, out_ref, d, me, send_sem, recv_sem).start()
-
-    out_ref[me] = sent[me]
+                to_peer(sent, came, d, me, send_sem, recv_sem).start()
+
+    came[me] = sent[me]
     for d in range(shards):
         @pl.when(d != me)
         def _():
-            from_peer(sent, out_ref, d, send_sem, recv_sem).wait()
-
-
-def packed_filter_kernel(groups, imgs, per_shard, in_ref, noise_ref, out_ref, *scratch):
-    shards, step = in_ref.shape[0], in_ref.shape[1] // 2
+            from_peer(sent, came, d, send_sem, recv_sem).wait()
+
     coef, ids = [], []
     for t in range(shards // PACK):
-        blocks = [in_ref[t * PACK + peer].astype(jnp.float32) for peer in range(PACK)]
+        blocks = [came[t * PACK + peer].astype(jnp.float32) for peer in range(PACK)]
         coef.append(unpack([block[:step] for block in blocks]))
         row = blocks[0][step:step + 1]
         for peer in range(1, PACK):
@@ -312,46 +311,31 @@
     noise = jnp.zeros((1, LANES), jnp.float32)
     for g in range(groups):
         noise = jnp.where(group == g, noise_ref[g], noise)
+    imgs = shards * images
     done = filter_lanes(groups, imgs, coef, kid * groups + ids, kid, noise, *scratch)
     for t in range(shards // PACK):
         for peer, block in enumerate(pack(done[:, t * 128:(t + 1) * 128])):
-            out_ref[t * PACK + peer] = block.astype(jnp.bfloat16)
-
-
-def restore_kernel(
-    per_shard, in_ref, table_hbm, bessel_hbm, out_hbm,
-    table_ref, bess, out_ref, held, sem, out_sem, send_sem, recv_sem,
-):
-    shards = in_ref.shape[0]
-    images = out_ref.shape[0]
-    q, radii = bess.shape[1:]
-    me = lax.axis_index("img")
-    loads = [
-        pltpu.make_async_copy(table_hbm, table_ref, sem.at[0]),
-        pltpu.make_async_copy(bessel_hbm, bess, sem.at[1]),
-    ]
-    for load in loads:
-        load.start()
-    greet(shards, me)
-    for d in range(shards):
-        @pl.when(d != me)
-        def _():
-            to_peer(in_ref, held, d, me, send_sem, recv_sem).start()
-    held[me] = in_ref[me]
-    half = 2 * per_shard
+            d = t * PACK + peer
+            answer[d] = block.astype(jnp.bfloat16)
+
+            @pl.when(d != me)
+            def _():
+                to_peer(answer, held, d, me, send_sem2, recv_sem2).start()
+    held[me] = answer[me]
     span = per_shard * q
     keep = (
         lax.broadcasted_iota(jnp.int32, (SHARE, span), 0) % per_shard
         == lax.broadcasted_iota(jnp.int32, (SHARE, span), 1) // q
     )
-    for load in loads:
-        load.wait()
-    for d in range(shards):
-        @pl.when(d != me)
-        def _():
-            from_peer(in_ref, held, d, send_sem, recv_sem).wait()
     back = []
     for t in range(shards // PACK):
+        for peer in range(PACK):
+            d = t * PACK + peer
+
+            @pl.when(d != me)
+            def _():
+                from_peer(answer, held, d, send_sem2, recv_sem2).wait()
+
         tile = unpack([held[t * PACK + peer].astype(jnp.float32) for peer in range(PACK)])
         flat = jnp.transpose(tile)
         for peer in range(PACK):
@@ -372,12 +356,6 @@
         store.wait()
 
 
-def remote_params(n):
-    return pltpu.CompilerParams(
-        vmem_limit_bytes=32 * 1024 * 1024, collective_id=n, has_side_effects=True
-    )
-
-
 def packed_body(particles, whitening, ctf, group_id, noise_var, bessel):
     images, radii, angles = particles.shape
     freqs, q = bessel.shape[:2]
@@ -392,11 +370,11 @@
     table = jnp.asarray(table.reshape(2 * freqs, angles), dtype=jnp.bfloat16)
     hbm = pl.BlockSpec(memory_space=pltpu.HBM)
     smem = pl.BlockSpec(memory_space=pltpu.SMEM)
-    arrived = pl.pallas_call(
-        functools.partial(project_kernel, per_shard),
-        out_shape=jax.ShapeDtypeStruct((shards, 2 * step, 128), jnp.bfloat16),
-        in_specs=[smem, hbm, hbm, hbm, hbm, hbm],
-        out_specs=VM,
+    return pl.pallas_call(
+        functools.partial(fused_kernel, per_shard, groups),
+        out_shape=jax.ShapeDtypeStruct(particles.shape, jnp.bfloat16),
+        in_specs=[smem, smem, hbm, hbm, hbm, hbm, hbm],
+        out_specs=hbm,
         scratch_shapes=[
             pltpu.VMEM(particles.shape, jnp.bfloat16),
             pltpu.VMEM(table.shape, jnp.bfloat16),
@@ -404,40 +382,22 @@
             pltpu.VMEM((1, radii), jnp.float32),
             pltpu.VMEM(bessel.shape, jnp.bfloat16),
             pltpu.VMEM((shards, 2 * step, 128), jnp.bfloat16),
+            pltpu.VMEM((shards, 2 * step, 128), jnp.bfloat16),
+            pltpu.VMEM((shards, step, 128), jnp.bfloat16),
+            pltpu.VMEM((shards, step, 128), jnp.bfloat16),
+            pltpu.VMEM(particles.shape, jnp.bfloat16),
             pltpu.SemaphoreType.DMA((5,)),
-            pltpu.SemaphoreType.DMA((shards,)),
-            pltpu.SemaphoreType.DMA((shards,)),
-        ],
-        compiler_params=remote_params(0),
-        name="project",
-    )(group_id, particles, table, ctf, whitening[None, :], bessel)
-    filtered = pl.pallas_call(
-        functools.partial(packed_filter_kernel, groups, shards * images, per_shard),
-        out_shape=jax.ShapeDtypeStruct((shards, step, 128), jnp.bfloat16),
-        in_specs=[VM, smem],
-        out_specs=VM,
-        scratch_shapes=filter_scratch(q, shards * SHARE),
-        compiler_params=PARAMS,
-        name="wiener_filter",
-    )(arrived, noise_var)
-    return pl.pallas_call(
-        functools.partial(restore_kernel, per_shard),
-        out_shape=jax.ShapeDtypeStruct(particles.shape, jnp.bfloat16),
-        in_specs=[VM, hbm, hbm],
-        out_specs=hbm,
-        scratch_shapes=[
-            pltpu.VMEM(table.shape, jnp.bfloat16),
-            pltpu.VMEM(bessel.shape, jnp.bfloat16),
-            pltpu.VMEM(particles.shape, jnp.bfloat16),
-            pltpu.VMEM((shards, step, 128), jnp.bfloat16),
-            pltpu.SemaphoreType.DMA((2,)),
             pltpu.SemaphoreType.DMA((images,)),
             pltpu.SemaphoreType.DMA((shards,)),
             pltpu.SemaphoreType.DMA((shards,)),
-        ],
-        compiler_params=remote_params(1),
-        name="restore",
-    )(filtered, table, bessel)
+            pltpu.SemaphoreType.DMA((shards,)),
+            pltpu.SemaphoreType.DMA((shards,)),
+        ] + filter_scratch(q, shards * SHARE),
+        compiler_params=pltpu.CompilerParams(
+            vmem_limit_bytes=VMEM_LIMIT, collective_id=0, has_side_effects=True
+        ),
+        name="fused",
+    )(group_id, noise_var, particles, table, ctf, whitening[None, :], bessel)
 
 
 def body(particles, whitening, ctf, group_id, noise_var, bessel):

time: 47 us -> 39.5 us (0.84)
  local copies, waits for them, and re-layouts: 7.02 us -> 1.87 us
  Pallas kernels: 39.7 us -> 37.5 us
    unnamed x17 -> x1, local copies, waits for them, and re-layouts: 7.02 us -> 1.87 us
    pallas_call x3 -> x1, Pallas kernels: 39.7 us -> 37.5 us  [packed_body(): pl.pallas_call(functools.partial(fused_kernel, per_shard, groups), out_sh...]
where the time goes in v4:
time: 39.5 us; the launch traced here: 39.4 us
  Pallas kernels  37.5 us (95%)
  local copies, waits for them, and re-layouts  1.87 us (5%)
    pallas_call x1, Pallas kernels, packed_body(): pl.pallas_call(functools.partial(fused_kernel, per_shard, groups), out_sh...  37.5 us
    unnamed x1, local copies, waits for them, and re-layouts  1.87 us

profile of v4, /device:TPU:0, one launch (start us, length us, event | category | flops | bytes accessed | tf_op | source)
XLA Modules:
  0.0 39.4 jit_solution(10398739965373030990)
XLA Ops:
  0.0 37.5 %fused.1 = bf16[2,256,512]{2,1,0:T(8,128)(2,1)} custom-call(s32[2]{0:T(128)} %gid_ref.1, f32[8]{0:T(128)} %noise_ref.1, bf16[2,256,512]{2,1,0:T(8,128)(2,1)} %part_hbm.1, bf16[256,512]{1,0:T(8,128)(2,1)} %constant.2.clone.table_hbm, f32[8,256]{1,0:T(8,128)} %ctf_hbm.1, f32[1,256]{1,0:T(1,128)} %bitcast.1, bf16[128,64,256]{2,1,0:T(8,128)(2,1)} %bessel_hbm.1), custom_call_target="tpu_custom_call" | custom-call | tf_op jit(solution)/shard_map/fused/pallas_call | solution.py:373
  37.5 1.9 %copy.9 = bf16[2,256,512]{2,1,0:T(8,128)(2,1)} copy(bf16[2,256,512]{2,1,0:T(8,128)(2,1)} %fused.1) | data formatting | bytes 1048576

commit v5 on v4

--- a/solution.py
+++ b/solution.py
@@ -66,7 +66,7 @@
             a_ref[i] = acc
             return carry
 
-        lax.fori_loop(0, q, update, 0, unroll=4)
+        lax.fori_loop(0, q, update, 0, unroll=8)
         for t in range(TILE):
             a_ref[kb * TILE + t] = rows[t]
 
@@ -109,7 +109,7 @@
             a_ref[start + t] = total[t] + jnp.where(col == start + t, noise, 0.0)
         return carry
 
-    lax.fori_loop(0, q // TILE, gram, 0)
+    lax.fori_loop(0, q // TILE, gram, 0, unroll=2)
     sweep_all(a_ref, c_ref, v_ref, q)
     e_lo = jnp.where(low, member, 0.0).astype(jnp.bfloat16)
     e_hi = jnp.where(low, 0.0, member).astype(jnp.bfloat16)
@@ -126,7 +126,7 @@
         d_ref[pl.ds(start, TILE), :] = jnp.sum(prod, axis=1)
         return carry
 
-    lax.fori_loop(0, q // TILE, apply, 0)
+    lax.fori_loop(0, q // TILE, apply, 0, unroll=2)
     return d_ref[...]
 
 

time: 39.5 us -> 37.7 us (0.954)
  Pallas kernels: 37.5 us -> 35.6 us
    pallas_call x1, Pallas kernels: 37.5 us -> 35.6 us  [packed_body(): pl.pallas_call(functools.partial(fused_kernel, per_shard, groups), out_sh...]
where the time goes in v5:
time: 37.7 us; the launch traced here: 37.5 us
  Pallas kernels  35.6 us (94%)
  local copies, waits for them, and re-layouts  1.87 us (5%)
    pallas_call x1, Pallas kernels, packed_body(): pl.pallas_call(functools.partial(fused_kernel, per_shard, groups), out_sh...  35.6 us
    unnamed x1, local copies, waits for them, and re-layouts  1.87 us

profile of v5, /device:TPU:0, one launch (start us, length us, event | category | flops | bytes accessed | tf_op | source)
XLA Modules:
  0.0 37.5 jit_solution(7682252235545496874)
XLA Ops:
  0.0 35.6 %fused.1 = bf16[2,256,512]{2,1,0:T(8,128)(2,1)} custom-call(s32[2]{0:T(128)} %gid_ref.1, f32[8]{0:T(128)} %noise_ref.1, bf16[2,256,512]{2,1,0:T(8,128)(2,1)} %part_hbm.1, bf16[256,512]{1,0:T(8,128)(2,1)} %constant.2.clone.table_hbm, f32[8,256]{1,0:T(8,128)} %ctf_hbm.1, f32[1,256]{1,0:T(1,128)} %bitcast.1, bf16[128,64,256]{2,1,0:T(8,128)(2,1)} %bessel_hbm.1), custom_call_target="tpu_custom_call" | custom-call | tf_op jit(solution)/shard_map/fused/pallas_call | solution.py:373
  35.6 1.9 %copy.9 = bf16[2,256,512]{2,1,0:T(8,128)(2,1)} copy(bf16[2,256,512]{2,1,0:T(8,128)(2,1)} %fused.1) | data formatting | bytes 1048576
